TPU v7x, 32 devices: a whole 2x2x4 slice. The times are simulated.
32 devices in a mesh: col: 4 (over z), grp: 8 (over y, x, core).
Axes of the slice: x: 2, y: 2, z: 4, core: 2. Of those that a mesh axis runs over, the one named last changes fastest.
Arguments:
- table_rows: bfloat16 [8, 256, 256], P('grp', None, 'col'), may hold values from -1.5 to 1.5
- pool_index: int32 [8, 4, 1024], P('grp'), may hold values from 0 to 255
- bag_length: int32 [8, 1024], P('grp'), may hold values from 1 to 4
- table_slot: int32 [8], replicated, may hold values from 0 to 7, each once
- dense_input: bfloat16 [1024, 13], P('grp'), may hold values from -6 to 6
- bottom_weight: bfloat16 [13, 256], replicated, may hold values from -1.75 to 1.75
- top_weight: bfloat16 [292, 2048], P(None, 'col'), may hold values from -0.375 to 0.375
- out_weight: bfloat16 [2048], P('col'), may hold values from -0.125 to 0.125
- labels: int32 [1024], P('grp'), may hold values 0 or 1
Outputs:
- logits: float32 [1024], P('grp')
- grad_top: float32 [292, 2048], P(None, ('col', 'grp'))
- grad_out: float32 [2048], P(('col', 'grp'))
- grad_bottom: float32 [13, 256], replicated
- grad_rows: float32 [8, 256, 256], P('grp', None, 'col')
Inputs may be any that keep to these rules, and one draw needn't show every extreme that they name: `pool_index`: each entry names one of its table's 256 looked-up rows. `bag_length`: slots at or past a bag's length are unused. `table_slot`: every feature is held by exactly one shard.
All inputs are finite; a program needn't handle non-finite values. No bound on the sum of `labels` on one device may be relied on, other than what follows from the above.
Results may differ from a plain program's by a relative error of at most 0.0071.
Values may be sent and summed in bfloat16 or wider, within the bound.
A program may use at most 128 MiB of HBM per device.

v0:
```python
import jax
import jax.numpy as jnp
import numpy as np
from jax import lax
from jax.sharding import PartitionSpec as P


def count_block(index_block, length_block, uniq_count):
    slot_iota = lax.broadcasted_iota(jnp.int32, index_block.shape, 1)
    row_ids = jnp.where(slot_iota < length_block[:, None, :], index_block, -1)
    values = lax.broadcasted_iota(jnp.int32, (1, 1, uniq_count), 2)
    counts = jnp.zeros((index_block.shape[0], index_block.shape[2], uniq_count), jnp.bfloat16)
    for slot_index in range(index_block.shape[1]):
        counts = counts + jnp.where(row_ids[:, slot_index, :, None] == values, 1.0, 0.0).astype(
            jnp.bfloat16
        )
    return counts


def pair_table(fields):
    upper_a, upper_b = np.triu_indices(fields, 1)
    return upper_a * fields + upper_b


def silu_slope(values):
    sigma = jax.nn.sigmoid(values)
    return sigma * (1.0 + values * (1.0 - sigma))


def interact(vectors):
    fields = vectors.shape[0]
    gram_matrix = jnp.einsum("asc,bsc->abs", vectors, vectors, preferred_element_type=jnp.float32)
    return gram_matrix.reshape(fields * fields, -1)[pair_table(fields)]


def spread(dpairs, vectors):
    fields = vectors.shape[0]
    symmetric = (
        jnp.zeros((fields * fields, dpairs.shape[0]), jnp.bfloat16)
        .at[pair_table(fields)]
        .set(dpairs.T)
    )
    symmetric = symmetric.reshape(fields, fields, -1)
    symmetric = symmetric + jnp.transpose(symmetric, (1, 0, 2))
    return jnp.einsum("abs,bsc->asc", symmetric, vectors, preferred_element_type=jnp.float32)


def body(
    table_rows,
    pool_index,
    bag_length,
    table_slot,
    dense_input,
    bottom_weight,
    top_weight,
    out_weight,
    labels,
):
    tab_count, uniq_count, col_width = table_rows.shape
    bag_slots = pool_index.shape[1]
    samples = pool_index.shape[2]
    local_rows = dense_input.shape[0]
    emb_width = bottom_weight.shape[1]
    stride = min(1024, samples)
    nblocks = samples // stride
    index_blocks = jnp.transpose(
        pool_index.reshape(tab_count, bag_slots, nblocks, stride), (2, 0, 1, 3)
    )
    length_blocks = jnp.transpose(bag_length.reshape(tab_count, nblocks, stride), (1, 0, 2))

    def pool_one(inputs):
        counts = count_block(inputs[0], inputs[1], uniq_count)
        return jnp.einsum(
            "tbu,tuc->tbc", counts, table_rows, preferred_element_type=jnp.float32
        ).astype(jnp.bfloat16)

    pooled_blocks = lax.map(pool_one, (index_blocks, length_blocks))
    pooled = jnp.transpose(pooled_blocks, (1, 0, 2, 3)).reshape(tab_count, samples, col_width)
    inverse = jnp.argsort(table_slot)
    bottom_pre = jnp.dot(dense_input, bottom_weight, preferred_element_type=jnp.float32)
    bottom_out = jax.nn.silu(bottom_pre).astype(jnp.bfloat16)
    arrived = lax.all_to_all(pooled, "grp", split_axis=1, concat_axis=0, tiled=True)
    gathered = lax.all_gather(arrived, "col", axis=2, tiled=True)
    tables = jnp.take(gathered, inverse, axis=0)
    mine_pre, mine_out, mine_dense = (bottom_pre, bottom_out, dense_input)
    vectors = jnp.concatenate([mine_out[None], tables], axis=0)
    pair_values = interact(vectors)
    features = jnp.concatenate([mine_out.astype(jnp.float32), pair_values.T], axis=1).astype(
        jnp.bfloat16
    )
    hidden_pre = jnp.dot(features, top_weight, preferred_element_type=jnp.float32)
    hidden = jax.nn.silu(hidden_pre).astype(jnp.bfloat16)
    logits = lax.psum(jnp.dot(hidden, out_weight, preferred_element_type=jnp.float32), "col")
    dlogit = (jax.nn.sigmoid(logits) - labels.astype(jnp.float32)) / local_rows
    grad_out_part = jnp.dot(hidden.astype(jnp.float32).T, dlogit, precision=lax.Precision.HIGHEST)
    out_delta = (
        dlogit[:, None] * out_weight.astype(jnp.float32)[None, :] * silu_slope(hidden_pre)
    ).astype(jnp.bfloat16)
    grad_top_part = lax.dot_general(
        features, out_delta, (((0,), (0,)), ((), ())), preferred_element_type=jnp.float32
    )
    grad_top, grad_out = (
        lax.psum_scatter(grad_top_part, "grp", scatter_dimension=1, tiled=True),
        lax.psum_scatter(grad_out_part, "grp", scatter_dimension=0, tiled=True),
    )
    dfeatures = lax.psum(
        lax.dot_general(
            out_delta, top_weight, (((1,), (1,)), ((), ())), preferred_element_type=jnp.float32
        ),
        "col",
    )
    dpairs = dfeatures[:, emb_width:].astype(jnp.bfloat16)
    dvectors = spread(dpairs, vectors)
    dbottom = (dfeatures[:, :emb_width] + dvectors[0]) * silu_slope(mine_pre)
    bottom_part = jnp.dot(
        mine_dense.astype(jnp.float32).T, dbottom, precision=lax.Precision.HIGHEST
    )
    dtables = jnp.take(dvectors[1:], table_slot, axis=0)
    grad_bottom = lax.psum(bottom_part, "grp")
    own_cols = lax.dynamic_slice_in_dim(
        dtables, lax.axis_index("col") * col_width, col_width, 2
    ).astype(jnp.bfloat16)
    dpooled = lax.all_to_all(own_cols, "grp", split_axis=0, concat_axis=1, tiled=True)
    dpooled_blocks = jnp.transpose(
        dpooled.reshape(tab_count, nblocks, stride, col_width), (1, 0, 2, 3)
    )

    def accumulate(running, inputs):
        counts = count_block(inputs[0], inputs[1], uniq_count)
        return (
            running
            + jnp.einsum("tbu,tbc->tuc", counts, inputs[2], preferred_element_type=jnp.float32),
            None,
        )

    grad_rows, _ = lax.scan(
        accumulate,
        jnp.zeros((tab_count, uniq_count, col_width), jnp.float32),
        (index_blocks, length_blocks, dpooled_blocks),
    )
    return (logits, grad_top, grad_out, grad_bottom, grad_rows)


def solution(mesh):
    placed = (
        P("grp", None, "col"),
        P("grp", None, None),
        P("grp", None),
        P(),
        P("grp", None),
        P(),
        P(None, "col"),
        P("col"),
        P("grp"),
    )
    return jax.shard_map(
        body,
        mesh=mesh,
        in_specs=placed,
        out_specs=(
            P("grp"),
            P(None, ("col", "grp")),
            P(("col", "grp")),
            P(),
            P("grp", None, "col"),
        ),
        check_vma=False,
    )
```

profile of v0, /device:TPU:0, one launch (start us, length us, event | category | flops | bytes accessed | tf_op | source)
XLA Modules:
  0.0 135.9 jit_solution(1632583464363825362)
XLA Ops:
  8.0 0.8 fusion.29
  8.8 1.8 %fusion = bf16[1,1024,64]{1,2,0:T(8,128)(2,1)S(1)} fusion(s32[1024]{0:T(1024)S(1)} %bitcast.91, s32[1024]{0:T(1024)S(1)} %bitcast.93, s32[1024]{0:T(1024)S(1)} %bitcast.95, s32[1024]{0:T(1024)S(1)} %bitcast.89, bf16[1,256,64]{1,2,0:T(8,128)(2,1)} %param.13), kind=kOutput, calls=%fused_computation.7 | convolution fusion | flops 38862848 | bytes 180224 | tf_op jit(solution)/shard_map/while/body/eval_jaxpr/tbu,tuc->tbc/dot_general | solution.py:73
  10.7 0.4 copy.75
  11.1 0.5 broadcast.359
  11.6 2.4 %reduce = bf16[1024,64]{1,0:T(8,128)(2,1)S(1)} reduce(bf16[1024,1,64]{2,1,0:T(2,128)(2,1)S(1)} %bitcast.83, bf16[]{:T(256)} %broadcast.359), dimensions={1}, to_apply=%bitcast.68.reduce_sub_computation | reduce | bytes 262146
  14.0 0.9 reshape.452
  14.9 5.2 %all-to-all-start = ((bf16[8,2,4096]{2,1,0:T(2,128)(2,1)}), bf16[8,2,4096]{2,1,0:T(2,128)(2,1)S(1)}, u32[]{:S(2)}, u32[]{:S(2)}) async-start(bf16[8,2,4096]{2,1,0:T(2,128)(2,1)} %reshape.452), calls=%async_computation | async-start | bytes 262144 | tf_op jit(solution)/shard_map/all_to_all | solution.py:82
  20.1 1.0 sort.17
  21.2 0.2 multiply_convert_fusion.2
  21.5 0.1 copy.79
  21.6 0.6 dynamic-slice.2
  22.9 2.8 %all-to-all-done = bf16[8,2,4096]{2,1,0:T(2,128)(2,1)S(1)} async-done(((bf16[8,2,4096]{2,1,0:T(2,128)(2,1)}), bf16[8,2,4096]{2,1,0:T(2,128)(2,1)S(1)}, u32[]{:S(2)}, u32[]{:S(2)}) %all-to-all-start) | async-done | bytes 131104 | tf_op jit(solution)/shard_map/all_to_all | solution.py:82
  25.6 0.3 reshape.453
  25.9 0.3 copy.76
  26.3 15.8 %all_gather.3 = bf16[8,128,256]{1,0,2:T(8,128)(2,1)S(1)} all-gather(bf16[8,128,64]{1,0,2:T(8,128)(2,1)S(1)} %bitcast.85), channel_id=1, replica_groups=mesh['col'=4,'grp'=8] {'col'}, dimensions={2}, use_global_device_ids=true | all-gather | bytes 655360 | tf_op jit(solution)/shard_map/all_gather | solution.py:83
  42.1 0.3 copy.77
  42.4 0.6 gather_fusion
  43.0 0.3 copy_select_fusion
  43.4 0.6 convolution_bitcast_fusion
  43.9 0.5 copy.80
  44.4 0.6 gather_fusion.1
  45.0 0.1 copy.81
  45.2 0.2 fusion.26
  45.4 0.2 convolution_bitcast_fusion.3
  45.6 12.4 %psum.21 = f32[128]{0:T(128)S(1)} all-reduce(f32[128]{0:T(128)S(1)} %convolution_bitcast_fusion.3), channel_id=1, replica_groups=mesh['col'=4,'grp'=8] {'col'}, use_global_device_ids=true, to_apply=%region_1.2 | all-reduce | flops 128 | bytes 1024 | tf_op jit(solution)/shard_map/psum | solution.py:93
  58.1 1.3 fusion.25
  59.3 1.0 fusion.45
  60.3 0.0 reduce-scatter.2.cloned.1.call-start
  60.4 0.2 fusion.22
  60.6 0.3 reduce-scatter.2.cloned.1.call-update
  60.9 30.8 %all-reduce.4.cloned.1.call-done = f32[128,292]{1,0:T(8,128)} async-done(((f32[128,292]{1,0:T(8,128)}), f32[128,292]{1,0:T(8,128)}) %all-reduce.4.cloned.1.call-update) | async-done | bytes 149520 | tf_op jit(solution)/shard_map/psum | solution.py:106
  91.7 0.8 fusion.27
  92.5 0.1 copy.83
  92.6 0.7 scatter_custom_fusion
  93.3 0.5 copy.85
  93.8 0.5 copy.84
  94.3 0.5 fusion.1
  94.8 0.7 copy.99
  95.5 0.1 slice.58
  95.5 0.6 gather_fusion.2
  96.1 0.1 constant_dynamic-slice_fusion
  96.3 0.1 copy.90
  96.4 0.7 select_convert_fusion.4
  97.2 3.7 %all-to-all-start.1 = ((bf16[8,128,64]{1,2,0:T(8,128)(2,1)}), bf16[8,128,64]{1,2,0:T(8,128)(2,1)S(1)}, u32[]{:S(2)}, u32[]{:S(2)}) async-start(bf16[8,128,64]{1,2,0:T(8,128)(2,1)} %select_convert_fusion.4), calls=%async_computation.2 | async-start | bytes 262144 | tf_op jit(solution)/shard_map/all_to_all | solution.py:123
  100.8 0.2 convolution_bitcast_fusion.2
  101.0 25.5 %all-reduce.1 = (f32[512]{0:T(512)S(1)}, f32[13,256]{1,0:T(8,128)}) all-reduce(f32[512]{0:T(512)S(1)} %bitcast.97, f32[13,256]{1,0:T(8,128)S(1)} %convolution_bitcast_fusion.2), channel_id=3, replica_groups=mesh['col'=4,'grp'=8] {'grp'}, use_global_device_ids=true, to_apply=%region_3.4.clone | all-reduce | flops 3840 | bytes 30720
  126.5 0.6 dynamic-slice.3
  127.1 1.4 %convolution_bitcast_fusion.1 = f32[1,256,64]{1,2,0:T(8,128)} fusion(s32[1024]{0:T(1024)S(1)} %bitcast.92, s32[1024]{0:T(1024)S(1)} %bitcast.94, s32[1024]{0:T(1024)S(1)} %bitcast.96, s32[1024]{0:T(1024)S(1)} %bitcast.90, bf16[8,128,64]{1,2,0:T(8,128)(2,1)S(1)} %all-to-all-done.1), kind=kOutput, calls=%fused_computation.8 | convolution fusion | flops 38797312 | bytes 212992 | tf_op jit(solution)/shard_map/while/body/eval_jaxpr/tbu,tbc->tuc/dot_general | solution.py:132
  (39 shorter events, 0.3 us)
Async XLA Ops:
  8.0 37.2 %copy-start = (bf16[292,512]{1,0:T(8,128)(2,1)S(1)}, bf16[292,512]{1,0:T(8,128)(2,1)}, u32[]{:S(2)}) copy-start(bf16[292,512]{1,0:T(8,128)(2,1)} %param.19) | copy-start | bytes 897028
  8.8 11.3 %copy-start.6 = (s32[8]{0:T(128)S(1)}, s32[8]{0:T(128)}, u32[]{:S(2)}) copy-start(s32[8]{0:T(128)} %param.16) | copy-start | bytes 100
  8.8 12.3 %copy-start.4 = (bf16[13,256]{1,0:T(8,128)(2,1)S(1)}, bf16[13,256]{1,0:T(8,128)(2,1)}, u32[]{:S(2)}) copy-start(bf16[13,256]{1,0:T(8,128)(2,1)} %param.18) | copy-start | bytes 19972
  8.8 12.3 %copy-start.5 = (bf16[128,13]{0,1:T(8,128)(2,1)S(1)}, bf16[128,13]{0,1:T(8,128)(2,1)}, u32[]{:S(2)}) copy-start(bf16[128,13]{0,1:T(8,128)(2,1)} %param.17) | copy-start | bytes 9988
  10.7 10.7 %copy-start.3 = (s32[36]{0:T(128)S(1)}, s32[36]{0:T(128)}, u32[]{:S(2)}) copy-start(s32[36]{0:T(128)} %constant.98) | copy-start | bytes 436
  10.7 10.7 %copy-start.2 = (bf16[512]{0:T(512)(128)(2,1)S(1)}, bf16[512]{0:T(512)(128)(2,1)}, u32[]{:S(2)}) copy-start(bf16[512]{0:T(512)(128)(2,1)} %param.20) | copy-start | bytes 3076
  10.7 10.9 %copy-start.9 = (u32[32]{0:T(128)S(1)}, u32[32]{0:T(128)}, u32[]{:S(2)}) copy-start(u32[32]{0:T(128)} %constant.102) | copy-start | bytes 388
  14.9 10.7 %all-to-all-start = ((bf16[8,2,4096]{2,1,0:T(2,128)(2,1)}), bf16[8,2,4096]{2,1,0:T(2,128)(2,1)S(1)}, u32[]{:S(2)}, u32[]{:S(2)}) async-start(bf16[8,2,4096]{2,1,0:T(2,128)(2,1)} %reshape.452), calls=%async_computation | async-start | bytes 262144 | tf_op jit(solution)/shard_map/all_to_all | solution.py:82
  20.1 71.6 %all-reduce.4.cloned.1.call-start = ((), (), s32[]{:S(2)}) async-start(), calls=%async_computation.4 | async-start | bytes 393216 | tf_op jit(solution)/shard_map/psum | solution.py:106
  43.3 14.7 %copy-start.7 = (s32[128]{0:T(128)S(1)}, s32[128]{0:T(128)}, u32[]{:S(2)}) copy-start(s32[128]{0:T(128)} %param.21) | copy-start | bytes 1540
  58.0 2.6 %copy-start.8 = (f32[128]{0:T(128)}, f32[128]{0:T(128)S(1)}, u32[]{:S(2)}) copy-start(f32[128]{0:T(128)S(1)} %psum.21) | copy-start | bytes 1540
  60.3 68.1 %reduce-scatter.2.cloned.1.call-start = ((), (), s32[]{:S(2)}) async-start(), calls=%async_computation.3 | async-start | bytes 884736 | tf_op jit(solution)/shard_map/reduce_scatter | solution.py:103
  95.4 5.4 %copy-start.1 = (f32[128,292]{1,0:T(8,128)S(1)}, f32[128,292]{1,0:T(8,128)}, u32[]{:S(2)}) copy-start(f32[128,292]{1,0:T(8,128)} %all-reduce.4.cloned.1.call-done) | copy-start | bytes 448516
  97.2 29.9 %all-to-all-start.1 = ((bf16[8,128,64]{1,2,0:T(8,128)(2,1)}), bf16[8,128,64]{1,2,0:T(8,128)(2,1)S(1)}, u32[]{:S(2)}, u32[]{:S(2)}) async-start(bf16[8,128,64]{1,2,0:T(8,128)(2,1)} %select_convert_fusion.4), calls=%async_computation.2 | async-start | bytes 262144 | tf_op jit(solution)/shard_map/all_to_all | solution.py:123
Sparse Core Ops, SparseCore 0:
  60.5 31.1 all-reduce.3
Sparse Core Ops, SparseCore 1:
  64.5 31.3 reduce-scatter.1
where the time goes:
time: 136 us
  blocking collectives  53.7 us (39%)
  waiting for transfers between devices  33.8 us (25%)
  between operations  16.5 us (12%)
  local copies, waits for them, and re-layouts  10.1 us (7%)
  starting transfers between devices  8.91 us (7%)
  matrix products  7.6 us (6%)
  other arithmetic  5.25 us (4%)
    psum x1, waiting for transfers between devices, body(): lax.psum(lax.dot_general(out_delta, top_weight, (((1,), (1,)), ((), ())),...  30.8 us
    unnamed x1, blocking collectives  25.5 us
    all_gather x1, blocking collectives, body(): gathered = lax.all_gather(arrived, 'col', axis=2, tiled=True)  15.8 us
    psum x1, blocking collectives, body(): lax.psum(jnp.dot(hidden, out_weight, preferred_element_type=jnp.float32),...  12.4 us
    all_to_all x1, starting transfers between devices, body(): lax.all_to_all(pooled, 'grp', split_axis=1, concat_axis=0, tiled=True)  5.17 us
    all_to_all x1, starting transfers between devices, body(): lax.all_to_all(own_cols, 'grp', split_axis=0, concat_axis=1, tiled=True)  3.66 us
    unnamed x28, local copies, waits for them, and re-layouts  3.1 us
    all_to_all x1, waiting for transfers between devices, body(): lax.all_to_all(pooled, 'grp', split_axis=1, concat_axis=0, tiled=True)  2.75 us
  transfers between devices with their start and end apart: 4, of which 2 were waited for; matrix products, arithmetic and copies ran while one was open for 7% of the time, Pallas kernels for 0%

commit v1 on v0

--- a/solution.py
+++ b/solution.py
@@ -1,7 +1,11 @@
+import functools
+
 import jax
 import jax.numpy as jnp
 import numpy as np
 from jax import lax
+from jax.experimental import pallas as pl
+from jax.experimental.pallas import tpu as pltpu
 from jax.sharding import PartitionSpec as P
 
 
@@ -76,12 +80,16 @@
 
     pooled_blocks = lax.map(pool_one, (index_blocks, length_blocks))
     pooled = jnp.transpose(pooled_blocks, (1, 0, 2, 3)).reshape(tab_count, samples, col_width)
-    inverse = jnp.argsort(table_slot)
+    picks = (
+        lax.broadcasted_iota(jnp.int32, (table_slot.shape[0],) * 2, 0) == table_slot[None, :]
+    ).astype(jnp.bfloat16)
     bottom_pre = jnp.dot(dense_input, bottom_weight, preferred_element_type=jnp.float32)
     bottom_out = jax.nn.silu(bottom_pre).astype(jnp.bfloat16)
     arrived = lax.all_to_all(pooled, "grp", split_axis=1, concat_axis=0, tiled=True)
     gathered = lax.all_gather(arrived, "col", axis=2, tiled=True)
-    tables = jnp.take(gathered, inverse, axis=0)
+    tables = jnp.einsum(
+        "fk,ksc->fsc", picks, gathered, preferred_element_type=jnp.float32
+    ).astype(jnp.bfloat16)
     mine_pre, mine_out, mine_dense = (bottom_pre, bottom_out, dense_input)
     vectors = jnp.concatenate([mine_out[None], tables], axis=0)
     pair_values = interact(vectors)
@@ -115,7 +123,12 @@
     bottom_part = jnp.dot(
         mine_dense.astype(jnp.float32).T, dbottom, precision=lax.Precision.HIGHEST
     )
-    dtables = jnp.take(dvectors[1:], table_slot, axis=0)
+    dtables = jnp.einsum(
+        "fk,fsc->ksc",
+        picks,
+        dvectors[1:].astype(jnp.bfloat16),
+        preferred_element_type=jnp.float32,
+    )
     grad_bottom = lax.psum(bottom_part, "grp")
     own_cols = lax.dynamic_slice_in_dim(
         dtables, lax.axis_index("col") * col_width, col_width, 2
@@ -139,6 +152,321 @@
         (index_blocks, length_blocks, dpooled_blocks),
     )
     return (logits, grad_top, grad_out, grad_bottom, grad_rows)
+
+
+MESH = pl.DeviceIdType.MESH
+F32, BF16 = jnp.float32, jnp.bfloat16
+UNROLLED_PAIRS = 128
+
+
+def contract(left, right, left_dim, right_dim):
+    return lax.dot_general(
+        left, right, (((left_dim,), (right_dim,)), ((), ())), preferred_element_type=F32
+    )
+
+
+def up(count, unit):
+    return -(-count // unit) * unit
+
+
+def side_by_side(ref, count, rows):
+    return jnp.concatenate([ref[k, rows, :] for k in range(count)], axis=1)
+
+
+def split_rows(values, parts):
+    row = lax.broadcasted_iota(jnp.int32, (16, values.shape[1]), 0)
+    block = jnp.zeros((16, values.shape[1]), F32)
+    rest = values
+    for part in range(parts):
+        head = rest.astype(BF16).astype(F32)
+        block = jnp.where(row == part, head, block)
+        rest = rest - head
+    return block.astype(BF16)
+
+
+def kernel(
+    ncol, ngrp,
+    slot_ref, rows_ref, index_ref, length_ref, dense_ref, bottom_ref, top_ref, out_ref, label_ref,
+    logits_ref, grad_top_ref, grad_out_ref, grad_bottom_ref, grad_rows_ref,
+    counts, pool_out, pool_in, weight_pad, pre, bottoms, base, spread_out, vec, gram_in,
+    hid, logit_in, top_out, top_in, delta_out, delta_in, dvec, back_out, back_in, corner_in,
+    pool_s, pool_r, gram_s, gram_r, logit_s, logit_r, top_s, top_r,
+    delta_s, delta_r, back_s, back_r, corner_s, corner_r,
+):
+    col, grp = lax.axis_index("col"), lax.axis_index("grp")
+    uniq, width = rows_ref.shape[1], rows_ref.shape[2]
+    bag, samples = index_ref.shape[1], index_ref.shape[2]
+    local, dense = dense_ref.shape
+    emb = bottom_ref.shape[1]
+    hidden_count = top_ref.shape[1]
+    piece = hidden_count // ngrp
+    fields = ngrp + 1
+    pairs = [(a, b) for a in range(fields) for b in range(a + 1, fields)]
+    npairs = len(pairs)
+    pair_pad = up(npairs, 16)
+    dense_pad = up(dense, 16)
+
+    barrier = pltpu.get_barrier_semaphore()
+    for d in range(1, ngrp):
+        pl.semaphore_signal(
+            barrier, inc=1, device_id={"grp": lax.rem(grp + d, ngrp)}, device_id_type=MESH
+        )
+    for d in range(1, ncol):
+        pl.semaphore_signal(
+            barrier, inc=1, device_id={"col": lax.rem(col + d, ncol)}, device_id_type=MESH
+        )
+
+    def send(axis, count, here, source, target, send_sem, recv_sem):
+        copies = []
+        for d in range(1, count):
+            peer = lax.rem(here + d, count)
+            copy = pltpu.make_async_remote_copy(
+                src_ref=source(peer),
+                dst_ref=target.at[here],
+                send_sem=send_sem.at[d],
+                recv_sem=recv_sem.at[d],
+                device_id={axis: peer},
+                device_id_type=MESH,
+            )
+            copy.start()
+            copies.append(copy)
+        return copies
+
+    def arrived(copies):
+        for copy in copies:
+            copy.wait_recv()
+
+    picks = (
+        lax.broadcasted_iota(jnp.int32, (dense_pad, dense), 0)
+        == lax.broadcasted_iota(jnp.int32, (dense_pad, dense), 1)
+    ).astype(F32).astype(BF16)
+    dense_t = contract(picks, dense_ref[...], 1, 1).astype(BF16)
+    ids = lax.broadcasted_iota(jnp.int32, (uniq, local), 0)
+    rows_bf = rows_ref[0]
+    for k in range(ngrp):
+        lanes = slice(k * local, (k + 1) * local)
+        total = jnp.zeros((uniq, local), F32)
+        for j in range(bag):
+            wanted = jnp.where(j < length_ref[:, lanes], index_ref[0, j : j + 1, lanes], -1)
+            total = total + jnp.where(ids == wanted, 1.0, 0.0)
+        counts[:, lanes] = total.astype(BF16)
+        pool_out[k, :width, :] = contract(rows_bf, counts[:, lanes], 0, 0).astype(BF16)
+        pool_out[k, width:, :] = dense_t
+    pl.semaphore_wait(barrier, ngrp - 1 + ncol - 1)
+    pool_copies = send("grp", ngrp, grp, lambda p: pool_out.at[p], pool_in, pool_s, pool_r)
+    pool_in[grp] = pool_out[grp]
+
+    weight_pad[...] = jnp.zeros_like(weight_pad)
+    weight_pad[:dense, :] = bottom_ref[...]
+    weight = weight_pad[...]
+    pre[...] = contract(weight, dense_t, 0, 0)
+    bottom = jax.nn.silu(pre[...]).astype(BF16)
+    spread_out[:emb, :] = bottom
+    spread_out[emb:, :] = jnp.zeros((pair_pad, local), BF16)
+    base[...] = contract(top_ref[:emb, :], bottom, 0, 0)
+    own = pl.ds(pl.multiple_of(col * width, width), width)
+    vec[0] = spread_out[own, :].astype(F32)
+    out_column = contract(out_ref[...], jnp.ones((1, local), BF16), 0, 0)
+    back_out[:, width:, :] = jnp.zeros((ngrp, dense_pad, local), BF16)
+    top_out[:, piece + pair_pad :, :] = jnp.zeros((ngrp, 16, local), BF16)
+    delta_out[:, width:, :] = jnp.zeros((ncol, pair_pad, local), BF16)
+
+    holders = []
+    for f in range(ngrp):
+        holder = jnp.int32(0)
+        for k in range(ngrp):
+            holder = jnp.where(slot_ref[k] == f, k, holder)
+        holders.append(holder)
+    arrived(pool_copies)
+    for f in range(ngrp):
+        vec[1 + f] = pool_in[holders[f], :width, :].astype(F32)
+    for i, (a, b) in enumerate(pairs):
+        gram_in[col, i : i + 1, :] = jnp.sum(vec[a] * vec[b], axis=0, keepdims=True)
+    gram_copies = send("col", ncol, col, lambda p: gram_in.at[col], gram_in, gram_s, gram_r)
+
+    for k in range(ngrp):
+        bottoms[:, k * local : (k + 1) * local] = jax.nn.silu(
+            contract(weight, pool_in[k, width:, :], 0, 0)
+        ).astype(BF16)
+
+    arrived(gram_copies)
+    gram = gram_in[0, :npairs, :]
+    for c in range(1, ncol):
+        gram = gram + gram_in[c, :npairs, :]
+    spread_out[emb : emb + npairs, :] = gram.astype(BF16)
+    pair_t = spread_out[emb : emb + npairs, :]
+    hidden_pre = base[...] + contract(top_ref[emb:, :], pair_t, 0, 0)
+    sigma = jax.nn.sigmoid(hidden_pre)
+    hid[...] = (hidden_pre * sigma).astype(BF16)
+    logit_in[col, :, :] = jnp.broadcast_to(
+        contract(out_ref[...], hid[...], 1, 0), (8, local)
+    )
+    logit_copies = send("col", ncol, col, lambda p: logit_in.at[col], logit_in, logit_s, logit_r)
+    base[...] = out_column * (sigma * (1.0 + hidden_pre * (1.0 - sigma)))
+    for k in range(ngrp):
+        top_out[k, piece : piece + pair_pad, :] = spread_out[emb:, :]
+    arrived(logit_copies)
+    logits = logit_in[0, 0:1, :]
+    for c in range(1, ncol):
+        logits = logits + logit_in[c, 0:1, :]
+    logits_ref[...] = logits
+    dlogit = (jax.nn.sigmoid(logits) - label_ref[...].astype(F32)) / local
+    delta = (dlogit * base[...]).astype(BF16)
+    dfeatures = contract(top_ref[...], delta, 1, 0)
+    for c in range(ncol):
+        delta_out[c, :width, :] = dfeatures[c * width : (c + 1) * width, :].astype(BF16)
+        delta_out[c, width : width + npairs, :] = dfeatures[emb:, :].astype(BF16)
+    delta_copies = send(
+        "col", ncol, col, lambda p: delta_out.at[p], delta_in, delta_s, delta_r
+    )
+    delta_in[col] = delta_out[col]
+    dlogit_rows = split_rows(dlogit, 3)
+    for k in range(ngrp):
+        top_out[k, :piece, :] = delta[k * piece : (k + 1) * piece, :]
+        share = contract(dlogit_rows, hid[k * piece : (k + 1) * piece, :], 1, 1)
+        top_out[k, piece + pair_pad :, :piece] = split_rows(
+            jnp.sum(share, axis=0, keepdims=True), 3
+        )
+    top_copies = send("grp", ngrp, grp, lambda p: top_out.at[p], top_in, top_s, top_r)
+    top_in[grp] = top_out[grp]
+
+    own_pre = pre[own, :]
+    own_sigma = jax.nn.sigmoid(own_pre)
+    own_slope = own_sigma * (1.0 + own_pre * (1.0 - own_sigma))
+    arrived(delta_copies)
+    arriving = delta_in[0].astype(F32)
+    for c in range(1, ncol):
+        arriving = arriving + delta_in[c].astype(F32)
+    dpairs = arriving[width:, :].astype(BF16).astype(F32)
+    where = {}
+    for i, (a, b) in enumerate(pairs):
+        where[a, b] = where[b, a] = i
+    for a in range(fields):
+        total = jnp.zeros((width, local), F32)
+        for b in range(fields):
+            if a != b:
+                i = where[a, b]
+                total = total + dpairs[i : i + 1, :] * vec[b]
+        if a == 0:
+            dbottom = (arriving[:width, :] + total) * own_slope
+        else:
+            dvec[a - 1] = total.astype(BF16)
+    rest, bottom_part = dbottom, jnp.zeros((dense_pad, width), F32)
+    for part in range(3):
+        head = rest.astype(BF16)
+        bottom_part = bottom_part + contract(dense_t, head, 1, 1)
+        rest = rest - head.astype(F32)
+    bottom_part = bottom_part.astype(BF16)
+    for k in range(ngrp):
+        back_out[k, :width, :] = dvec[slot_ref[k]]
+        back_out[k, width:, :width] = bottom_part
+    back_copies = send("grp", ngrp, grp, lambda p: back_out.at[p], back_in, back_s, back_r)
+    back_in[grp] = back_out[grp]
+
+    arrived(top_copies)
+    deltas = side_by_side(top_in, ngrp, slice(0, piece))
+    grad_top_ref[:emb, :] = contract(bottoms[...], deltas, 1, 1)
+    grad_top_ref[emb:, :] = contract(
+        side_by_side(top_in, ngrp, slice(piece, piece + pair_pad)), deltas, 1, 1
+    )[:npairs, :]
+    out_rows = top_in[0, piece + pair_pad :, :].astype(F32)
+    for k in range(1, ngrp):
+        out_rows = out_rows + top_in[k, piece + pair_pad :, :].astype(F32)
+    grad_out_ref[...] = jnp.sum(out_rows, axis=0, keepdims=True)[:, :piece]
+
+    arrived(back_copies)
+    corner = back_in[0, width:, :].astype(F32)
+    for k in range(1, ngrp):
+        corner = corner + back_in[k, width:, :].astype(F32)
+    corner_in[col] = corner
+    corner_copies = send(
+        "col", ncol, col, lambda p: corner_in.at[col], corner_in, corner_s, corner_r
+    )
+    grad_rows_ref[0] = contract(
+        counts[...], side_by_side(back_in, ngrp, slice(0, width)), 1, 1
+    )
+    arrived(corner_copies)
+    grad_bottom_ref[...] = jnp.concatenate(
+        [corner_in[c, :dense, :width] for c in range(ncol)], axis=1
+    )
+    for copies in (
+        pool_copies, gram_copies, logit_copies, delta_copies, top_copies, back_copies, corner_copies
+    ):
+        for copy in copies:
+            copy.wait_send()
+
+
+def fused(ncol, ngrp, table_rows, pool_index, bag_length, table_slot, dense_input, bottom_weight,
+          top_weight, out_weight, labels):
+    uniq, width = table_rows.shape[1:]
+    samples = pool_index.shape[2]
+    local, dense = dense_input.shape
+    emb = bottom_weight.shape[1]
+    topin, hidden_count = top_weight.shape
+    piece = hidden_count // ngrp
+    npairs = topin - emb
+    pair_pad, dense_pad = up(npairs, 16), up(dense, 16)
+    shape = jax.ShapeDtypeStruct
+    vmem = pl.BlockSpec(memory_space=pltpu.VMEM)
+    dma = pltpu.SemaphoreType.DMA
+    sems = []
+    for count in (ngrp, ncol, ncol, ngrp, ncol, ngrp, ncol):
+        sems += [dma((count,)), dma((count,))]
+    made = pl.pallas_call(
+        functools.partial(kernel, ncol, ngrp),
+        out_shape=(
+            shape((1, local), F32),
+            shape((topin, piece), F32),
+            shape((1, piece), F32),
+            shape((dense, emb), F32),
+            shape((1, uniq, width), F32),
+        ),
+        in_specs=[pl.BlockSpec(memory_space=pltpu.SMEM)] + [vmem] * 8,
+        out_specs=(vmem,) * 5,
+        scratch_shapes=[
+            pltpu.VMEM((uniq, samples), BF16),
+            pltpu.VMEM((ngrp, width + dense_pad, local), BF16),
+            pltpu.VMEM((ngrp, width + dense_pad, local), BF16),
+            pltpu.VMEM((dense_pad, emb), BF16),
+            pltpu.VMEM((emb, local), F32),
+            pltpu.VMEM((emb, samples), BF16),
+            pltpu.VMEM((hidden_count, local), F32),
+            pltpu.VMEM((emb + pair_pad, local), BF16),
+            pltpu.VMEM((ngrp + 1, width, local), F32),
+            pltpu.VMEM((ncol, up(npairs, 8), local), F32),
+            pltpu.VMEM((hidden_count, local), BF16),
+            pltpu.VMEM((ncol, 8, local), F32),
+            pltpu.VMEM((ngrp, piece + pair_pad + 16, local), BF16),
+            pltpu.VMEM((ngrp, piece + pair_pad + 16, local), BF16),
+            pltpu.VMEM((ncol, width + pair_pad, local), BF16),
+            pltpu.VMEM((ncol, width + pair_pad, local), BF16),
+            pltpu.VMEM((ngrp, width, local), BF16),
+            pltpu.VMEM((ngrp, width + dense_pad, local), BF16),
+            pltpu.VMEM((ngrp, width + dense_pad, local), BF16),
+            pltpu.VMEM((ncol, dense_pad, local), F32),
+        ] + sems,
+        compiler_params=pltpu.CompilerParams(
+            collective_id=0, has_side_effects=True, vmem_limit_bytes=32 * 2**20
+        ),
+    )(
+        table_slot, table_rows, pool_index, bag_length, dense_input, bottom_weight, top_weight,
+        out_weight.reshape(1, -1), labels.reshape(1, -1),
+    )
+    logits, grad_top, grad_out, grad_bottom, grad_rows = made
+    return logits.reshape(-1), grad_top, grad_out.reshape(-1), grad_bottom, grad_rows
+
+
+def choose(ncol, ngrp, *arrays):
+    table_rows, dense_input, top_weight = arrays[0], arrays[4], arrays[6]
+    local, width, piece = dense_input.shape[0], table_rows.shape[2], top_weight.shape[1] // ngrp
+    fits = (
+        table_rows.shape[0] == 1
+        and (ngrp + 1) * ngrp // 2 <= UNROLLED_PAIRS
+        and local % 128 == 0
+        and width % 16 == 0 and width <= local
+        and piece % 16 == 0 and piece <= local
+    )
+    return fused(ncol, ngrp, *arrays) if fits else body(*arrays)
 
 
 def solution(mesh):
@@ -154,7 +482,7 @@
         P("grp"),
     )
     return jax.shard_map(
-        body,
+        functools.partial(choose, mesh.shape["col"], mesh.shape["grp"]),
         mesh=mesh,
         in_specs=placed,
         out_specs=(

time: 136 us -> 37.3 us (0.27)
  blocking collectives: 53.7 us -> 0 us
  waiting for transfers between devices: 33.8 us -> 0 us
  Pallas kernels: 0 us -> 30.7 us
  between operations: 16.5 us -> 0.72 us
  starting transfers between devices: 8.91 us -> 0 us
  matrix products: 7.6 us -> 0 us
  other arithmetic: 5.25 us -> 0 us
  local copies, waits for them, and re-layouts: 10.1 us -> 5.58 us
    psum x1 -> x0, waiting for transfers between devices: 30.8 us -> none  [body(): lax.psum(lax.dot_general(out_delta, top_weight, (((1,), (1,)), ((), ())),...]
    pallas_call x0 -> x1, Pallas kernels: none -> 30.7 us  [fused(): pl.pallas_call(functools.partial(kernel, ncol, ngrp), out_shape=(shape((1...]
    unnamed x1 -> x0, blocking collectives: 25.5 us -> none
    all_gather x1 -> x0, blocking collectives: 15.8 us -> none  [body(): gathered = lax.all_gather(arrived, 'col', axis=2, tiled=True)]
    psum x1 -> x0, blocking collectives: 12.4 us -> none  [body(): lax.psum(jnp.dot(hidden, out_weight, preferred_element_type=jnp.float32),...]
    all_to_all x2 -> x0, starting transfers between devices: 8.83 us -> none  [the longest x1 5.17 us: body(): lax.all_to_all(pooled, 'grp', split_axis=1, concat_axis=0, tiled=True)]
    dot_general x11 -> x0, matrix products: 7.6 us -> none  [the longest x1 1.84 us: pool_one(): jnp.einsum('tbu,tuc->tbc', counts, table_rows, preferred_element_type=jnp...]
    all_to_all x2 -> x0, waiting for transfers between devices: 2.76 us -> none  [the longest x1 2.75 us: body(): lax.all_to_all(pooled, 'grp', split_axis=1, concat_axis=0, tiled=True)]
  transfers between devices with their start and end apart: 4 -> 0, of which waited for: 2 -> 0; matrix products, arithmetic and copies ran while one was open for 7% -> 0% of each run, Pallas kernels for 0% -> 0%
where the time goes in v1:
time: 37.3 us; the launch traced here: 37 us
  Pallas kernels  30.7 us (82%)
  local copies, waits for them, and re-layouts  5.58 us (15%)
  between operations  0.72 us (2%)
    pallas_call x1, Pallas kernels, fused(): pl.pallas_call(functools.partial(kernel, ncol, ngrp), out_shape=(shape((1...  30.7 us
    unnamed x23, local copies, waits for them, and re-layouts  4.88 us

profile of v1, /device:TPU:0, one launch (start us, length us, event | category | flops | bytes accessed | tf_op | source)
XLA Modules:
  0.0 37.0 jit_solution(17901587744316754158)
XLA Ops:
  0.6 0.0 copy-start.7
  0.6 0.0 copy-start.6
  0.7 0.7 %reshape.22.out_ref = bf16[1,512]{1,0:T(2,128)(2,1)S(1)} reshape(bf16[512]{0:T(512)(128)(2,1)} %param.16) | data formatting | bytes 2048 | tf_op jit(solution)/shard_map/reshape | solution.py:453
  1.3 0.0 copy-done.7
  1.3 0.1 copy.15.dense_ref
  1.5 0.0 copy-done.6
  1.5 0.0 copy-start.1
  1.5 0.0 copy-start.2
  1.5 0.0 copy-start.3
  1.5 0.0 copy-start.4
  1.5 0.0 copy-start.5
  1.5 0.1 copy.14.rows_ref
  1.7 0.5 %copy-done.1 = s32[1,4,1024]{2,1,0:T(4,128)S(1)} copy-done((s32[1,4,1024]{2,1,0:T(4,128)S(1)}, s32[1,4,1024]{2,1,0:T(4,128)}, u32[]{:S(2)}) %copy-start.1) | copy-done | bytes 16408
  2.2 0.0 copy-done.2
  2.2 0.0 copy-done.3
  2.2 0.0 copy-done.4
  2.2 0.0 copy-done.5
  2.2 0.0 copy-start
  2.2 1.0 %copy-done = bf16[292,512]{1,0:T(8,128)(2,1)S(1)} copy-done((bf16[292,512]{1,0:T(8,128)(2,1)S(1)}, bf16[292,512]{1,0:T(8,128)(2,1)}, u32[]{:S(2)}) %copy-start) | copy-done | bytes 299032
  3.2 30.7 %shard_map.128 = (f32[1,128]{1,0:T(1,128)S(1)}, f32[292,64]{1,0:T(8,128)S(1)}, f32[1,64]{1,0:T(1,128)S(1)}, f32[13,256]{1,0:T(8,128)S(1)}, f32[1,256,64]{2,1,0:T(8,128)S(1)}) custom-call(s32[8]{0:T(128)S(1)} %copy-done.4, bf16[1,256,64]{2,1,0:T(8,128)(2,1)S(1)} %copy.14.rows_ref, s32[1,4,1024]{2,1,0:T(4,128)S(1)} %copy-done.1, s32[1,1024]{1,0:T(1,128)S(1)} %copy-done.3, ...), custom_call_target="tpu_custom_call" | custom-call | tf_op jit(solution)/shard_map/pallas_call | solution.py:415
  33.9 0.7 %copy.17 = f32[1,256,64]{1,2,0:T(8,128)} copy(f32[1,256,64]{2,1,0:T(8,128)S(1)} %get-tuple-element.19) | data formatting | bytes 131072
  34.6 0.8 %copy.16 = f32[292,64]{0,1:T(8,128)} copy(f32[292,64]{1,0:T(8,128)S(1)} %get-tuple-element.16) | data formatting | bytes 149504
  35.3 0.5 %copy.21 = f32[128]{0:T(128)} copy(f32[128]{0:T(128)S(1)} %bitcast.5) | data formatting | bytes 1024
  35.8 0.5 %copy.22 = f32[64]{0:T(128)} copy(f32[64]{0:T(128)S(1)} %bitcast.4) | data formatting | bytes 512
  36.4 0.6 %copy.23 = f32[13,256]{1,0:T(8,128)} copy(f32[13,256]{1,0:T(8,128)S(1)} %get-tuple-element.28) | data formatting | bytes 26624
Async XLA Ops:
  0.6 0.7 %copy-start.7 = (bf16[128,13]{0,1:T(8,128)(2,1)S(1)}, bf16[128,13]{0,1:T(8,128)(2,1)}, u32[]{:S(2)}) copy-start(bf16[128,13]{0,1:T(8,128)(2,1)} %param.13) | copy-start | bytes 9988
  0.6 0.8 %copy-start.6 = (bf16[1,256,64]{1,2,0:T(8,128)(2,1)S(1)}, bf16[1,256,64]{1,2,0:T(8,128)(2,1)}, u32[]{:S(2)}) copy-start(bf16[1,256,64]{1,2,0:T(8,128)(2,1)} %param.9) | copy-start | bytes 98308
  1.5 0.7 %copy-start.1 = (s32[1,4,1024]{2,1,0:T(4,128)S(1)}, s32[1,4,1024]{2,1,0:T(4,128)}, u32[]{:S(2)}) copy-start(s32[1,4,1024]{2,1,0:T(4,128)} %index_ref.1) | copy-start | bytes 49156
  1.5 0.7 %copy-start.2 = (bf16[13,256]{1,0:T(8,128)(2,1)S(1)}, bf16[13,256]{1,0:T(8,128)(2,1)}, u32[]{:S(2)}) copy-start(bf16[13,256]{1,0:T(8,128)(2,1)} %bottom_ref.1) | copy-start | bytes 19972
  1.5 0.7 %copy-start.3 = (s32[1,1024]{1,0:T(1,128)S(1)}, s32[1,1024]{1,0:T(1,128)}, u32[]{:S(2)}) copy-start(s32[1,1024]{1,0:T(1,128)} %length_ref.1) | copy-start | bytes 12292
  1.5 0.7 %copy-start.4 = (s32[8]{0:T(128)S(1)}, s32[8]{0:T(128)}, u32[]{:S(2)}) copy-start(s32[8]{0:T(128)} %slot_ref.1) | copy-start | bytes 100
  1.5 0.7 %copy-start.5 = (s32[128]{0:T(128)S(1)}, s32[128]{0:T(128)}, u32[]{:S(2)}) copy-start(s32[128]{0:T(128)} %param.17) | copy-start | bytes 1540
  2.2 1.0 %copy-start = (bf16[292,512]{1,0:T(8,128)(2,1)S(1)}, bf16[292,512]{1,0:T(8,128)(2,1)}, u32[]{:S(2)}) copy-start(bf16[292,512]{1,0:T(8,128)(2,1)} %top_ref.1) | copy-start | bytes 897028

commit v2 on v1

--- a/solution.py
+++ b/solution.py
@@ -186,17 +186,17 @@
 
 def kernel(
     ncol, ngrp,
-    slot_ref, rows_ref, index_ref, length_ref, dense_ref, bottom_ref, top_ref, out_ref, label_ref,
+    slot_ref, rows_ref, index_ref, length_ref, dense_ref, bottom_ref, top_hbm, out_ref, label_ref,
     logits_ref, grad_top_ref, grad_out_ref, grad_bottom_ref, grad_rows_ref,
     counts, pool_out, pool_in, weight_pad, pre, bottoms, base, spread_out, vec, gram_in,
-    hid, logit_in, top_out, top_in, delta_out, delta_in, dvec, back_out, back_in, corner_in,
-    pool_s, pool_r, gram_s, gram_r, logit_s, logit_r, top_s, top_r,
-    delta_s, delta_r, back_s, back_r, corner_s, corner_r,
+    hid, top_out, top_in, delta_out, delta_in, dvec, back_out, back_in, corner_in,
+    pool_s, pool_r, gram_s, gram_r, delta_s, delta_r,
+    top_s, top_r, back_s, back_r, corner_s, corner_r, top_ref, load_sem, dense_rows,
 ):
     col, grp = lax.axis_index("col"), lax.axis_index("grp")
-    uniq, width = rows_ref.shape[1], rows_ref.shape[2]
+    width, uniq = rows_ref.shape[1], rows_ref.shape[2]
     bag, samples = index_ref.shape[1], index_ref.shape[2]
-    local, dense = dense_ref.shape
+    dense, local = dense_ref.shape
     emb = bottom_ref.shape[1]
     hidden_count = top_ref.shape[1]
     piece = hidden_count // ngrp
@@ -206,6 +206,8 @@
     pair_pad = up(npairs, 16)
     dense_pad = up(dense, 16)
 
+    top_load = pltpu.make_async_copy(top_hbm, top_ref, load_sem)
+    top_load.start()
     barrier = pltpu.get_barrier_semaphore()
     for d in range(1, ngrp):
         pl.semaphore_signal(
@@ -236,11 +238,10 @@
         for copy in copies:
             copy.wait_recv()
 
-    picks = (
-        lax.broadcasted_iota(jnp.int32, (dense_pad, dense), 0)
-        == lax.broadcasted_iota(jnp.int32, (dense_pad, dense), 1)
-    ).astype(F32).astype(BF16)
-    dense_t = contract(picks, dense_ref[...], 1, 1).astype(BF16)
+    out_row = out_ref[...].reshape(1, hidden_count)
+    dense_rows[...] = jnp.zeros_like(dense_rows)
+    dense_rows[:dense, :] = dense_ref[...]
+    dense_t = dense_rows[...]
     ids = lax.broadcasted_iota(jnp.int32, (uniq, local), 0)
     rows_bf = rows_ref[0]
     for k in range(ngrp):
@@ -250,7 +251,7 @@
             wanted = jnp.where(j < length_ref[:, lanes], index_ref[0, j : j + 1, lanes], -1)
             total = total + jnp.where(ids == wanted, 1.0, 0.0)
         counts[:, lanes] = total.astype(BF16)
-        pool_out[k, :width, :] = contract(rows_bf, counts[:, lanes], 0, 0).astype(BF16)
+        pool_out[k, :width, :] = contract(rows_bf, counts[:, lanes], 1, 0).astype(BF16)
         pool_out[k, width:, :] = dense_t
     pl.semaphore_wait(barrier, ngrp - 1 + ncol - 1)
     pool_copies = send("grp", ngrp, grp, lambda p: pool_out.at[p], pool_in, pool_s, pool_r)
@@ -263,13 +264,14 @@
     bottom = jax.nn.silu(pre[...]).astype(BF16)
     spread_out[:emb, :] = bottom
     spread_out[emb:, :] = jnp.zeros((pair_pad, local), BF16)
+    top_load.wait()
     base[...] = contract(top_ref[:emb, :], bottom, 0, 0)
     own = pl.ds(pl.multiple_of(col * width, width), width)
     vec[0] = spread_out[own, :].astype(F32)
-    out_column = contract(out_ref[...], jnp.ones((1, local), BF16), 0, 0)
+    out_column = contract(out_row, jnp.ones((1, local), BF16), 0, 0)
     back_out[:, width:, :] = jnp.zeros((ngrp, dense_pad, local), BF16)
     top_out[:, piece + pair_pad :, :] = jnp.zeros((ngrp, 16, local), BF16)
-    delta_out[:, width:, :] = jnp.zeros((ncol, pair_pad, local), BF16)
+    delta_out[:, width : width + pair_pad, :] = jnp.zeros((ncol, pair_pad, local), BF16)
 
     holders = []
     for f in range(ngrp):
@@ -298,38 +300,19 @@
     hidden_pre = base[...] + contract(top_ref[emb:, :], pair_t, 0, 0)
     sigma = jax.nn.sigmoid(hidden_pre)
     hid[...] = (hidden_pre * sigma).astype(BF16)
-    logit_in[col, :, :] = jnp.broadcast_to(
-        contract(out_ref[...], hid[...], 1, 0), (8, local)
-    )
-    logit_copies = send("col", ncol, col, lambda p: logit_in.at[col], logit_in, logit_s, logit_r)
     base[...] = out_column * (sigma * (1.0 + hidden_pre * (1.0 - sigma)))
     for k in range(ngrp):
         top_out[k, piece : piece + pair_pad, :] = spread_out[emb:, :]
-    arrived(logit_copies)
-    logits = logit_in[0, 0:1, :]
-    for c in range(1, ncol):
-        logits = logits + logit_in[c, 0:1, :]
-    logits_ref[...] = logits
-    dlogit = (jax.nn.sigmoid(logits) - label_ref[...].astype(F32)) / local
-    delta = (dlogit * base[...]).astype(BF16)
-    dfeatures = contract(top_ref[...], delta, 1, 0)
+    dfeatures = contract(top_ref[...], base[...].astype(BF16), 1, 0)
+    logit_rows = split_rows(contract(out_row, hid[...], 1, 0), 3)
     for c in range(ncol):
         delta_out[c, :width, :] = dfeatures[c * width : (c + 1) * width, :].astype(BF16)
         delta_out[c, width : width + npairs, :] = dfeatures[emb:, :].astype(BF16)
+        delta_out[c, width + pair_pad :, :] = logit_rows
     delta_copies = send(
         "col", ncol, col, lambda p: delta_out.at[p], delta_in, delta_s, delta_r
     )
     delta_in[col] = delta_out[col]
-    dlogit_rows = split_rows(dlogit, 3)
-    for k in range(ngrp):
-        top_out[k, :piece, :] = delta[k * piece : (k + 1) * piece, :]
-        share = contract(dlogit_rows, hid[k * piece : (k + 1) * piece, :], 1, 1)
-        top_out[k, piece + pair_pad :, :piece] = split_rows(
-            jnp.sum(share, axis=0, keepdims=True), 3
-        )
-    top_copies = send("grp", ngrp, grp, lambda p: top_out.at[p], top_in, top_s, top_r)
-    top_in[grp] = top_out[grp]
-
     own_pre = pre[own, :]
     own_sigma = jax.nn.sigmoid(own_pre)
     own_slope = own_sigma * (1.0 + own_pre * (1.0 - own_sigma))
@@ -337,7 +320,10 @@
     arriving = delta_in[0].astype(F32)
     for c in range(1, ncol):
         arriving = arriving + delta_in[c].astype(F32)
-    dpairs = arriving[width:, :].astype(BF16).astype(F32)
+    logits = jnp.sum(arriving[width + pair_pad :, :], axis=0, keepdims=True)
+    logits_ref[...] = logits
+    dlogit = (jax.nn.sigmoid(logits) - label_ref[...].astype(F32)) / local
+    dpairs = (arriving[width : width + pair_pad, :] * dlogit).astype(BF16).astype(F32)
     where = {}
     for i, (a, b) in enumerate(pairs):
         where[a, b] = where[b, a] = i
@@ -348,7 +334,7 @@
                 i = where[a, b]
                 total = total + dpairs[i : i + 1, :] * vec[b]
         if a == 0:
-            dbottom = (arriving[:width, :] + total) * own_slope
+            dbottom = (arriving[:width, :] * dlogit + total) * own_slope
         else:
             dvec[a - 1] = total.astype(BF16)
     rest, bottom_part = dbottom, jnp.zeros((dense_pad, width), F32)
@@ -363,12 +349,23 @@
     back_copies = send("grp", ngrp, grp, lambda p: back_out.at[p], back_in, back_s, back_r)
     back_in[grp] = back_out[grp]
 
+    delta = (dlogit * base[...]).astype(BF16)
+    dlogit_rows = split_rows(dlogit, 3)
+    for k in range(ngrp):
+        top_out[k, :piece, :] = delta[k * piece : (k + 1) * piece, :]
+        share = contract(dlogit_rows, hid[k * piece : (k + 1) * piece, :], 1, 1)
+        top_out[k, piece + pair_pad :, :piece] = split_rows(
+            jnp.sum(share, axis=0, keepdims=True), 3
+        )
+    top_copies = send("grp", ngrp, grp, lambda p: top_out.at[p], top_in, top_s, top_r)
+    top_in[grp] = top_out[grp]
+
     arrived(top_copies)
     deltas = side_by_side(top_in, ngrp, slice(0, piece))
-    grad_top_ref[:emb, :] = contract(bottoms[...], deltas, 1, 1)
-    grad_top_ref[emb:, :] = contract(
-        side_by_side(top_in, ngrp, slice(piece, piece + pair_pad)), deltas, 1, 1
-    )[:npairs, :]
+    grad_top_ref[:, :emb] = contract(deltas, bottoms[...], 1, 1)
+    grad_top_ref[:, emb:] = contract(
+        deltas, side_by_side(top_in, ngrp, slice(piece, piece + pair_pad)), 1, 1
+    )[:, :npairs]
     out_rows = top_in[0, piece + pair_pad :, :].astype(F32)
     for k in range(1, ngrp):
         out_rows = out_rows + top_in[k, piece + pair_pad :, :].astype(F32)
@@ -383,17 +380,23 @@
         "col", ncol, col, lambda p: corner_in.at[col], corner_in, corner_s, corner_r
     )
     grad_rows_ref[0] = contract(
-        counts[...], side_by_side(back_in, ngrp, slice(0, width)), 1, 1
+        side_by_side(back_in, ngrp, slice(0, width)), counts[...], 1, 1
     )
     arrived(corner_copies)
     grad_bottom_ref[...] = jnp.concatenate(
         [corner_in[c, :dense, :width] for c in range(ncol)], axis=1
     )
     for copies in (
-        pool_copies, gram_copies, logit_copies, delta_copies, top_copies, back_copies, corner_copies
+        pool_copies, gram_copies, delta_copies, top_copies, back_copies, corner_copies
     ):
         for copy in copies:
             copy.wait_send()
+
+
+def hand_over(*refs):
+    half = len(refs) // 2
+    for made, result in zip(refs[:half], refs[half:]):
+        result[...] = made[...]
 
 
 def fused(ncol, ngrp, table_rows, pool_index, bag_length, table_slot, dense_input, bottom_weight,
@@ -410,18 +413,19 @@
     vmem = pl.BlockSpec(memory_space=pltpu.VMEM)
     dma = pltpu.SemaphoreType.DMA
     sems = []
-    for count in (ngrp, ncol, ncol, ngrp, ncol, ngrp, ncol):
+    for count in (ngrp, ncol, ncol, ngrp, ngrp, ncol):
         sems += [dma((count,)), dma((count,))]
     made = pl.pallas_call(
         functools.partial(kernel, ncol, ngrp),
         out_shape=(
             shape((1, local), F32),
-            shape((topin, piece), F32),
+            shape((piece, topin), F32),
             shape((1, piece), F32),
             shape((dense, emb), F32),
-            shape((1, uniq, width), F32),
+            shape((1, width, uniq), F32),
         ),
-        in_specs=[pl.BlockSpec(memory_space=pltpu.SMEM)] + [vmem] * 8,
+        in_specs=[pl.BlockSpec(memory_space=pltpu.SMEM)] + [vmem] * 5
+        + [pl.BlockSpec(memory_space=pltpu.HBM)] + [vmem] * 2,
         out_specs=(vmem,) * 5,
         scratch_shapes=[
             pltpu.VMEM((uniq, samples), BF16),
@@ -435,25 +439,37 @@
             pltpu.VMEM((ngrp + 1, width, local), F32),
             pltpu.VMEM((ncol, up(npairs, 8), local), F32),
             pltpu.VMEM((hidden_count, local), BF16),
-            pltpu.VMEM((ncol, 8, local), F32),
             pltpu.VMEM((ngrp, piece + pair_pad + 16, local), BF16),
             pltpu.VMEM((ngrp, piece + pair_pad + 16, local), BF16),
-            pltpu.VMEM((ncol, width + pair_pad, local), BF16),
-            pltpu.VMEM((ncol, width + pair_pad, local), BF16),
+            pltpu.VMEM((ncol, width + pair_pad + 16, local), BF16),
+            pltpu.VMEM((ncol, width + pair_pad + 16, local), BF16),
             pltpu.VMEM((ngrp, width, local), BF16),
             pltpu.VMEM((ngrp, width + dense_pad, local), BF16),
             pltpu.VMEM((ngrp, width + dense_pad, local), BF16),
             pltpu.VMEM((ncol, dense_pad, local), F32),
-        ] + sems,
+        ] + sems + [
+            pltpu.VMEM((topin, hidden_count), BF16),
+            pltpu.SemaphoreType.DMA,
+            pltpu.VMEM((dense_pad, local), BF16),
+        ],
         compiler_params=pltpu.CompilerParams(
-            collective_id=0, has_side_effects=True, vmem_limit_bytes=32 * 2**20
+            collective_id=0, has_side_effects=True, vmem_limit_bytes=60 * 2**20
         ),
     )(
-        table_slot, table_rows, pool_index, bag_length, dense_input, bottom_weight, top_weight,
-        out_weight.reshape(1, -1), labels.reshape(1, -1),
-    )
-    logits, grad_top, grad_out, grad_bottom, grad_rows = made
-    return logits.reshape(-1), grad_top, grad_out.reshape(-1), grad_bottom, grad_rows
+        table_slot, jnp.swapaxes(table_rows, 1, 2), pool_index, bag_length, dense_input.T,
+        bottom_weight, top_weight, out_weight, labels.reshape(1, -1),
+    )
+    logits, grad_top, grad_out, grad_bottom, grad_rows = pl.pallas_call(
+        hand_over,
+        out_shape=tuple(shape(a.shape, a.dtype) for a in made),
+        in_specs=[vmem] * 5,
+        out_specs=(vmem,) * 5,
+        compiler_params=pltpu.CompilerParams(vmem_limit_bytes=60 * 2**20),
+    )(*made)
+    return (
+        logits.reshape(-1), grad_top.T, grad_out.reshape(-1), grad_bottom,
+        jnp.swapaxes(grad_rows, 1, 2),
+    )
 
 
 def choose(ncol, ngrp, *arrays):

time: 37.3 us -> 31.8 us (0.85)
  local copies, waits for them, and re-layouts: 5.58 us -> 0 us
    unnamed x23 -> x0, local copies, waits for them, and re-layouts: 4.88 us -> none
    pallas_call x0 -> x1, Pallas kernels: none -> 1.6 us  [fused(): pl.pallas_call(hand_over, out_shape=tuple((shape(a.shape, a.dtype) for a...]
    pallas_call x1, Pallas kernels: 30.7 us -> 29.4 us  [fused(): pl.pallas_call(functools.partial(kernel, ncol, ngrp), out_shape=(shape((1...]
    reshape x1 -> x0, local copies, waits for them, and re-layouts: 0.69 us -> none  [fused(): out_weight.reshape(1, -1)]
where the time goes in v2:
time: 31.8 us; the launch traced here: 31.6 us
  Pallas kernels  31 us (97%)
  between operations  0.64 us (2%)
    pallas_call x1, Pallas kernels, fused(): pl.pallas_call(functools.partial(kernel, ncol, ngrp), out_shape=(shape((1...  29.4 us
    pallas_call x1, Pallas kernels, fused(): pl.pallas_call(hand_over, out_shape=tuple((shape(a.shape, a.dtype) for a...  1.6 us

profile of v2, /device:TPU:0, one launch (start us, length us, event | category | flops | bytes accessed | tf_op | source)
XLA Modules:
  0.0 31.6 jit_solution(14476866565262746837)
XLA Ops:
  0.6 29.4 %shard_map.128 = (f32[1,128]{1,0:T(1,128)}, f32[64,292]{1,0:T(8,128)}, f32[1,64]{1,0:T(1,128)}, f32[13,256]{1,0:T(8,128)}, f32[1,64,256]{2,1,0:T(8,128)}) custom-call(s32[8]{0:T(128)} %slot_ref.1, bf16[1,64,256]{2,1,0:T(8,128)(2,1)} %bitcast.7, s32[1,4,1024]{2,1,0:T(4,128)} %index_ref.1, s32[1,1024]{1,0:T(1,128)} %length_ref.1, bf16[13,128]{1,0:T(8,128)(2,1)} %bitcast.8, ...), custom_call_target="tpu_custom_call" | custom-call | tf_op jit(solution)/shard_map/pallas_call | solution.py:418
  30.0 1.6 %shard_map.129 = (f32[1,128]{1,0:T(1,128)}, f32[64,292]{1,0:T(8,128)}, f32[1,64]{1,0:T(1,128)}, f32[13,256]{1,0:T(8,128)}, f32[1,64,256]{2,1,0:T(8,128)}) custom-call(f32[1,128]{1,0:T(1,128)} %get-tuple-element.15.refs_0_, f32[64,292]{1,0:T(8,128)} %get-tuple-element.16.refs_1_, f32[1,64]{1,0:T(1,128)} %get-tuple-element.17.refs_2_, ...), custom_call_target="tpu_custom_call" | custom-call | tf_op jit(solution)/shard_map/pallas_call | solution.py:462
